TPU v7x, 512 devices: a whole 4x4x16 slice. The times are simulated.
512 devices in a mesh: dom: 64 (over x, z), head: 8 (over y, core).
Axes of the slice: x: 4, y: 4, z: 16, core: 2. Of those that a mesh axis runs over, the one named last changes fastest.
Arguments:
- node_feats: bfloat16 [65536, 512], P(('dom', 'head')), may hold values from -6 to 6
- norm_gain: float32 [512], replicated, may hold values from 0.25 to 1.75
- w_qkv: bfloat16 [512, 1536], P(None, 'head'), may hold values from -1 to 1
- w_out: bfloat16 [512, 512], replicated, may hold values from -0.25 to 0.25
- rand_feat: float32 [8, 64, 256], P('head'), may hold values from -6 to 6
- temper: float32 [8], P('head'), may hold values from 1 to 6
- edge_src: int32 [512, 6], P('dom'), may hold values from 0 to 511, as said below
- edge_count: int32 [512], P('dom'), may hold values from 1 to 6, as said below
- block_fill: int32 [512], replicated, may hold values from 32 to 128, as said below
Outputs:
- update: bfloat16 [65536, 512], P(('dom', 'head'))
Inputs may be any that keep to these rules, and one draw needn't show every extreme that they name: `edge_src`: destination block b lies in partition p = b // 8; each of its source blocks lies in partition p - 1, p or p + 1; slot 0 holds b itself, and slots at or beyond edge_count[b] hold b. `edge_count`: every block of some partition uses all 6 slots. `block_fill`: block 0 is full.
All inputs are finite; a program needn't handle non-finite values.
Results may differ from a plain program's by a relative error of at most 0.012.
The roundings to bfloat16 on the way count: a program that leaves them out, or rounds other values in their place, can miss the bound.
Values may be sent and summed in bfloat16 or wider, within the bound.
A program may use at most 64 MiB of HBM per device.

v0:
```python
import math
import jax
import jax.numpy as jnp
from jax import lax
from jax.sharding import PartitionSpec as P

BLK = 128


def padded(block, sides, width):
    for axis, dim in sides:
        count = lax.axis_size(axis)
        forward = [(i, i + 1) for i in range(count - 1)]
        backward = [(target, source) for source, target in forward]
        low = lax.ppermute(
            lax.slice_in_dim(block, block.shape[dim] - width, None, axis=dim), axis, forward
        )
        high = lax.ppermute(lax.slice_in_dim(block, 0, width, axis=dim), axis, backward)
        block = jnp.concatenate([low, block, high], axis=dim)
    return block


def layer_norm(rows, gain):
    widened = rows.astype(jnp.float32)
    centred = widened - jnp.mean(widened, axis=-1, keepdims=True)
    spread = jnp.mean(centred * centred, axis=-1, keepdims=True)
    return (centred * lax.rsqrt(spread + 1e-05) * gain).astype(jnp.bfloat16)


def features(rows, directions, temper):
    head_dim = rows.shape[-1]
    scaled = rows.astype(jnp.float32) * (jnp.sqrt(temper)[None, :, None] * head_dim ** (-0.25))
    lifted = jnp.einsum("nhd,hdm->nhm", scaled, directions, precision=lax.Precision.HIGHEST)
    return jnp.exp(
        lifted - 0.5 * jnp.sum(scaled * scaled, axis=-1, keepdims=True)
    ) * directions.shape[2] ** (-0.5)


def shards(
    node_feats, norm_gain, w_qkv, w_out, rand_feat, temper, edge_src, edge_count, block_fill
):
    groups = lax.axis_size("head")
    heads_here = rand_feat.shape[0]
    head_dim = rand_feat.shape[1]
    part_rows = node_feats.shape[0] * groups
    blocks = part_rows // BLK
    slots = edge_src.shape[1]
    domain = lax.axis_index("dom")
    normed = layer_norm(node_feats, norm_gain)
    qkv = jnp.dot(
        lax.all_gather(normed, "head", axis=0, tiled=True),
        w_qkv,
        preferred_element_type=jnp.float32,
    ).astype(jnp.bfloat16)
    split = qkv.reshape(part_rows, heads_here, 3, head_dim)
    queries = split[:, :, 0]
    own_fill = lax.dynamic_slice_in_dim(block_fill, domain * blocks, blocks)
    lanes = lax.broadcasted_iota(jnp.int32, (blocks, BLK), 1)
    valid = (lanes < own_fill[:, None]).astype(jnp.float32).reshape(part_rows)
    phi_keys = features(split[:, :, 1], rand_feat, temper) * valid[:, None, None]
    partial_sum = jnp.einsum(
        "nhm,nhe->hme",
        phi_keys,
        split[:, :, 2].astype(jnp.float32),
        precision=lax.Precision.HIGHEST,
    )
    kernel_sum, key_total = lax.psum((partial_sum, jnp.sum(phi_keys, axis=0)), "dom")
    pairs = split[:, :, 1:].reshape(part_rows, heads_here * 2 * head_dim)
    widened = padded(pairs, (("dom", 0),), part_rows)
    kv_blocks = widened.reshape(3 * blocks, BLK, heads_here, 2, head_dim)
    key_blocks = kv_blocks[:, :, :, 0]
    value_blocks = kv_blocks[:, :, :, 1]
    local_src = edge_src - (domain - 1) * blocks
    scale = head_dim ** (-0.5)
    per_step = math.gcd(blocks, max(1, 8 // heads_here))
    turns = blocks // per_step
    width = slots * BLK
    q_steps = queries.reshape(turns, per_step, BLK, heads_here, head_dim)
    src_steps = local_src.reshape(turns, per_step, slots)
    id_steps = edge_src.reshape(turns, per_step, slots)
    count_steps = edge_count.reshape(turns, per_step)

    def attend_all(packed):
        q_part, src_part, id_part, count_part = packed
        keys = jnp.take(key_blocks, src_part, axis=0).reshape(per_step, width, heads_here, head_dim)
        values = jnp.take(value_blocks, src_part, axis=0).reshape(
            per_step, width, heads_here, head_dim
        )
        fills = jnp.take(block_fill, id_part)
        slot_ids = lax.broadcasted_iota(jnp.int32, (per_step, slots, BLK), 1)
        lane_ids = lax.broadcasted_iota(jnp.int32, (per_step, slots, BLK), 2)
        allowed = ((lane_ids < fills[:, :, None]) & (slot_ids < count_part[:, None, None])).reshape(
            per_step, width
        )
        scores = (
            jnp.einsum("bqhd,bkhd->bhqk", q_part, keys, preferred_element_type=jnp.float32) * scale
        )
        scores = jnp.where(allowed[:, None, None, :], scores, -1e30)
        row_max = jnp.max(scores, axis=3, keepdims=True)
        weights = jnp.exp(scores - row_max)
        total = jnp.sum(weights, axis=3)
        accum = jnp.einsum(
            "bhqk,bkhd->bqhd",
            weights.astype(jnp.bfloat16),
            values,
            preferred_element_type=jnp.float32,
        )
        return accum / jnp.transpose(total, (0, 2, 1))[..., None]

    local = lax.map(attend_all, (q_steps, src_steps, id_steps, count_steps))
    local = local.reshape(part_rows, heads_here, head_dim)
    phi_queries = features(queries, rand_feat, temper)
    numer = jnp.einsum("nhm,hme->nhe", phi_queries, kernel_sum, precision=lax.Precision.HIGHEST)
    denom = jnp.einsum("nhm,hm->nh", phi_queries, key_total, precision=lax.Precision.HIGHEST)
    mixed = (
        (local + numer / denom[..., None])
        .astype(jnp.bfloat16)
        .reshape(part_rows, heads_here * head_dim)
    )
    returned = lax.all_to_all(mixed, "head", split_axis=0, concat_axis=1, tiled=True)
    return jnp.dot(returned, w_out, preferred_element_type=jnp.float32).astype(jnp.bfloat16)


def solution(mesh):
    return jax.shard_map(
        shards,
        mesh=mesh,
        in_specs=(
            P(("dom", "head"), None),
            P(),
            P(None, "head"),
            P(),
            P("head", None, None),
            P("head"),
            P("dom", None),
            P("dom"),
            P(),
        ),
        out_specs=P(("dom", "head"), None),
        check_vma=False,
    )
```

profile of v0, /device:TPU:1, one launch (start us, length us, event | category | flops | bytes accessed | tf_op | source)
XLA Modules:
  0.0 337.9 jit_solution(1613953993842794324)
XLA Ops:
  6.5 0.0 all-gather.2.cloned.1.call-start
  6.6 1.1 convert_reduce_fusion
  7.7 1.1 fusion.31
  8.8 1.7 fusion.33
  10.5 0.0 all-gather.2.cloned.1.call-update
  10.5 0.0 all-reduce.2.cloned.1.call-start
  10.6 1.3 compare_and_fusion
  11.8 0.1 reshape.313
  11.9 0.7 compare_select_fusion.1
  12.6 0.1 reshape.298
  12.7 0.8 gather_fusion
  13.5 0.1 reshape.297
  13.6 0.1 copy.20
  14.4 0.1 dynamic_slice.14
  14.5 0.1 select_bitcast_fusion
  14.6 0.1 fusion.44
  14.6 33.0 %all-gather.2.cloned.1.call-done = bf16[1024,512]{1,0:T(8,128)(2,1)} async-done(((bf16[128,512]{1,0:T(8,128)(2,1)}), bf16[1024,512]{1,0:T(8,128)(2,1)}) %all-gather.2.cloned.1.call-update) | async-done | bytes 1048592 | tf_op jit(solution)/shard_map/all_gather | solution.py:51
  47.6 1.7 convolution_convert_fusion
  49.4 3.0 collective-permute-start
  52.4 1.3 collective-permute-start.1
  53.7 0.1 multiply_reduce_fusion
  53.9 1.3 fusion.48
  55.1 1.1 fusion.27
  56.2 1.1 fusion.12
  57.4 0.7 copy.30
  58.1 0.0 all-reduce.2.cloned.1.call-update
  58.1 117.4 %psum.15 = f32[256]{0:T(256)S(1)} all-reduce(f32[256]{0:T(256)S(1)} %get-tuple-element.43), channel_id=1, replica_groups=mesh['dom'=64,'head'=8] {'dom'}, use_global_device_ids=true, to_apply=%region_8.10 | all-reduce | flops 256 | bytes 2048 | tf_op jit(solution)/shard_map/psum | solution.py:67
  175.5 1.0 fusion.49
  176.5 0.0 collective-permute-done.1
  176.5 0.1 maximum_bitcast_fusion
  176.6 0.2 copy.29
  176.7 0.1 fusion.47
  176.8 0.2 copy_bitcast_fusion
  177.0 0.7 gather_fusion.1
  177.7 0.7 gather_fusion.2
  178.4 1.8 broadcast_select_fusion
  180.2 0.6 copy.22
  180.7 0.9 reshape.266
  181.6 1.7 copy.19
  183.3 1.8 reshape.264
  185.1 0.7 fusion
  185.8 0.9 fusion.1
  186.8 1.0 fusion.24
  187.7 0.2 copy.24
  187.9 120.0 %all-reduce.2.cloned.1.call-done = f32[256,64]{0,1:T(8,128)} async-done(((f32[256,64]{0,1:T(8,128)}), f32[256,64]{0,1:T(8,128)}) %all-reduce.2.cloned.1.call-update) | async-done | bytes 65552 | tf_op jit(solution)/shard_map/psum | solution.py:67
  307.9 2.0 fusion.20
  309.9 20.3 %all_to_all.19 = bf16[8,128,64]{1,2,0:T(8,128)(2,1)S(1)} all-to-all(bf16[8,128,64]{1,2,0:T(8,128)(2,1)S(1)} %copy.26), channel_id=1, replica_groups=mesh['dom'=64,'head'=8] {'head'}, dimensions={0} | all-to-all | bytes 262144 | tf_op jit(solution)/shard_map/all_to_all | solution.py:120
  330.2 0.9 convolution_convert_fusion.1
  (29 shorter events, 0.1 us)
Async XLA Ops:
  6.5 323.6 %copy-start = (bf16[512,512]{1,0:T(8,128)(2,1)S(1)}, bf16[512,512]{1,0:T(8,128)(2,1)}, u32[]{:S(2)}) copy-start(bf16[512,512]{1,0:T(8,128)(2,1)} %param.14) | copy-start | bytes 1572868
  6.5 7.1 %copy-start.6 = (s32[8,6]{1,0:T(8,128)S(1)}, s32[8,6]{1,0:T(8,128)}, u32[]{:S(2)}) copy-start(s32[8,6]{1,0:T(8,128)} %param.17) | copy-start | bytes 580
  6.5 6.2 %copy-start.1 = (s32[512]{0:T(512)S(1)}, s32[512]{0:T(512)}, u32[]{:S(2)}) copy-start(s32[512]{0:T(512)} %param.19) | copy-start | bytes 6148
  6.5 8.0 %copy-start.7 = (s32[8]{0:T(128)S(1)}, s32[8]{0:T(128)}, u32[]{:S(2)}) copy-start(s32[8]{0:T(128)} %param.18) | copy-start | bytes 100
  6.5 41.1 %copy-start.5 = (bf16[512,192]{0,1:T(8,128)(2,1)S(1)}, bf16[512,192]{0,1:T(8,128)(2,1)}, u32[]{:S(2)}) copy-start(bf16[512,192]{0,1:T(8,128)(2,1)} %param.13) | copy-start | bytes 589828
  6.5 41.1 %all-gather.2.cloned.1.call-start = ((), (), s32[]{:S(2)}) async-start(), calls=%async_computation.1 | async-start | bytes 1179648 | tf_op jit(solution)/shard_map/all_gather | solution.py:51
  10.5 297.3 %all-reduce.2.cloned.1.call-start = ((), (), s32[]{:S(2)}) async-start(), calls=%async_computation.2 | async-start | bytes 131072 | tf_op jit(solution)/shard_map/psum | solution.py:67
  12.7 41.1 %copy-start.4 = (f32[1,64,256]{2,1,0:T(8,128)S(1)}, f32[1,64,256]{2,1,0:T(8,128)}, u32[]{:S(2)}) copy-start(f32[1,64,256]{2,1,0:T(8,128)} %param.15) | copy-start | bytes 196612
  49.4 127.1 %collective-permute-start = (bf16[1024,128]{0,1:T(8,128)(2,1)S(1)}, bf16[1024,128]{0,1:T(8,128)(2,1)S(1)}, u32[]{:S(2)}, u32[]{:S(2)}) collective-permute-start(bf16[1024,128]{0,1:T(8,128)(2,1)S(1)} %bitcast.148), channel_id=1, source_target_pairs={{0,8},{8,16},{16,24},{24,32},{32,40},{40,48},{48,56},{56,64},{64,7... | collective-permute-start | bytes 786440 | tf_op jit(solution)/shard_map/ppermute | solution.py:15
  52.4 124.1 %collective-permute-start.1 = (bf16[1024,128]{0,1:T(8,128)(2,1)S(1)}, bf16[1024,128]{0,1:T(8,128)(2,1)S(1)}, u32[]{:S(2)}, u32[]{:S(2)}) collective-permute-start(bf16[1024,128]{0,1:T(8,128)(2,1)S(1)} %bitcast.149), channel_id=1, source_target_pairs={{8,0},{16,8},{24,16},{32,24},{40,32},{48,40},{56,48},{64,56},{72,6... | collective-permute-start | bytes 786440 | tf_op jit(solution)/shard_map/ppermute | solution.py:18
  180.7 4.4 %copy-start.3 = (bf16[8,8,8,128]{3,2,1,0:T(8,128)(2,1)S(1)}, bf16[8,8,8,128]{3,2,1,0:T(8,128)(2,1)}, u32[]{:S(2)}) copy-start(bf16[8,8,8,128]{3,2,1,0:T(8,128)(2,1)} %copy.30) | copy-start | bytes 393220
  185.1 1.6 copy-start.2
Sparse Core Ops, SparseCore 0:
  10.6 36.9 all-gather.1
  58.2 249.6 all-reduce.1
where the time goes:
time: 338 us
  waiting for transfers between devices  153 us (45%)
  blocking collectives  138 us (41%)
  between operations  14.4 us (4%)
  matrix products  10.7 us (3%)
  local copies, waits for them, and re-layouts  8.88 us (3%)
  other arithmetic  8.83 us (3%)
  starting transfers between devices  4.4 us (1%)
    psum x1, waiting for transfers between devices, shards(): lax.psum((partial_sum, jnp.sum(phi_keys, axis=0)), 'dom')  120 us
    psum x1, blocking collectives, shards(): lax.psum((partial_sum, jnp.sum(phi_keys, axis=0)), 'dom')  117 us
    all_gather x1, waiting for transfers between devices, shards(): lax.all_gather(normed, 'head', axis=0, tiled=True)  33 us
    all_to_all x1, blocking collectives, shards(): lax.all_to_all(mixed, 'head', split_axis=0, concat_axis=1, tiled=True)  20.3 us
  transfers between devices with their start and end apart: 4, of which 2 were waited for; matrix products, arithmetic and copies ran while one was open for 6% of the time, Pallas kernels for 0%

commit v1 on v0

--- a/solution.py
+++ b/solution.py
@@ -48,7 +48,9 @@
     domain = lax.axis_index("dom")
     normed = layer_norm(node_feats, norm_gain)
     qkv = jnp.dot(
-        lax.all_gather(normed, "head", axis=0, tiled=True),
+        jnp.concatenate(
+            lax.all_to_all(jnp.stack([normed] * lax.axis_size("head")), "head", 0, 0), axis=0
+        ),
         w_qkv,
         preferred_element_type=jnp.float32,
     ).astype(jnp.bfloat16)

time: 338 us -> 325 us (0.962)
  waiting for transfers between devices: 153 us -> 130 us
  starting transfers between devices: 4.4 us -> 13.1 us
    all_gather x1 -> x0, waiting for transfers between devices: 33 us -> none  [shards(): lax.all_gather(normed, 'head', axis=0, tiled=True)]
    all_to_all x0 -> x1, waiting for transfers between devices: none -> 12.4 us  [shards(): lax.all_to_all(jnp.stack([normed] * lax.axis_size('head')), 'head', 0, 0)]
    all_to_all x0 -> x1, starting transfers between devices: none -> 10.5 us  [shards(): lax.all_to_all(jnp.stack([normed] * lax.axis_size('head')), 'head', 0, 0)]
where the time goes in v1:
time: 325 us; the launch traced here: 324 us
  blocking collectives  140 us (43%)
  waiting for transfers between devices  130 us (40%)
  between operations  14.4 us (4%)
  starting transfers between devices  13.1 us (4%)
  local copies, waits for them, and re-layouts  9.95 us (3%)
  matrix products  9.52 us (3%)
  other arithmetic  6.78 us (2%)
    psum x1, blocking collectives, shards(): lax.psum((partial_sum, jnp.sum(phi_keys, axis=0)), 'dom')  120 us
    psum x1, waiting for transfers between devices, shards(): lax.psum((partial_sum, jnp.sum(phi_keys, axis=0)), 'dom')  118 us
    all_to_all x1, blocking collectives, shards(): lax.all_to_all(mixed, 'head', split_axis=0, concat_axis=1, tiled=True)  20.3 us
    all_to_all x1, waiting for transfers between devices, shards(): lax.all_to_all(jnp.stack([normed] * lax.axis_size('head')), 'head', 0, 0)  12.4 us
    all_to_all x1, starting transfers between devices, shards(): lax.all_to_all(jnp.stack([normed] * lax.axis_size('head')), 'head', 0, 0)  10.5 us
  transfers between devices with their start and end apart: 4, of which 2 were waited for; matrix products, arithmetic and copies ran while one was open for 6% of the time, Pallas kernels for 0%

profile of v1, /device:TPU:1, one launch (start us, length us, event | category | flops | bytes accessed | tf_op | source)
XLA Modules:
  0.0 324.4 jit_solution(11955356980267230117)
XLA Ops:
  6.5 1.1 convert_reduce_fusion
  7.6 1.1 fusion.31
  8.7 1.0 fusion.33
  9.8 1.1 stack.2
  10.8 10.5 %all-to-all-start = ((bf16[8,128,512]{2,1,0:T(8,128)(2,1)}), bf16[8,128,512]{2,1,0:T(8,128)(2,1)S(1)}, u32[]{:S(2)}, u32[]{:S(2)}) async-start(bf16[8,128,512]{2,1,0:T(8,128)(2,1)} %stack.2), calls=%async_computation | async-start | bytes 2097152 | tf_op jit(solution)/shard_map/all_to_all | solution.py:52
  21.3 0.6 compare_and_fusion
  21.9 0.1 reshape.304
  22.0 0.1 reshape.319
  22.1 0.8 gather_fusion
  22.9 0.1 reshape.303
  23.0 0.1 copy.20
  23.8 0.1 dynamic_slice.14
  23.9 0.1 select_bitcast_fusion
  23.9 0.1 fusion.44
  24.0 12.4 %all-to-all-done = bf16[8,128,512]{2,1,0:T(8,128)(2,1)S(1)} async-done(((bf16[8,128,512]{2,1,0:T(8,128)(2,1)}), bf16[8,128,512]{2,1,0:T(8,128)(2,1)S(1)}, u32[]{:S(2)}, u32[]{:S(2)}) %all-to-all-start) | async-done | bytes 1048608 | tf_op jit(solution)/shard_map/all_to_all | solution.py:52
  36.4 0.5 convolution_convert_fusion
  37.0 1.3 collective-permute-start
  38.3 1.3 collective-permute-start.1
  39.6 0.1 multiply_reduce_fusion
  39.7 1.3 fusion.48
  41.0 1.1 fusion.27
  42.1 1.1 fusion.12
  43.3 0.7 copy.30
  43.9 0.0 all-reduce.2.cloned.1.call-update
  44.0 120.2 %psum.15 = f32[256]{0:T(256)S(1)} all-reduce(f32[256]{0:T(256)S(1)} %get-tuple-element.43), channel_id=1, replica_groups=mesh['dom'=64,'head'=8] {'dom'}, use_global_device_ids=true, to_apply=%region_8.10 | all-reduce | flops 256 | bytes 2048 | tf_op jit(solution)/shard_map/psum | solution.py:69
  164.2 1.0 fusion.49
  165.1 0.0 collective-permute-done
  165.1 0.0 collective-permute-done.1
  165.1 0.1 maximum_bitcast_fusion
  165.2 0.2 copy.29
  165.4 0.1 fusion.47
  165.5 0.2 copy_bitcast_fusion
  165.6 0.7 gather_fusion.1
  166.4 0.7 gather_fusion.2
  167.1 1.8 broadcast_select_fusion
  168.8 0.6 copy.22
  169.4 0.0 copy-start.3
  169.4 0.9 reshape.272
  170.3 1.7 copy.19
  172.0 1.8 reshape.270
  173.8 0.7 fusion
  174.5 0.9 fusion.1
  175.4 1.0 fusion.24
  176.4 0.2 copy.24
  176.5 117.8 %all-reduce.2.cloned.1.call-done = f32[256,64]{0,1:T(8,128)} async-done(((f32[256,64]{0,1:T(8,128)}), f32[256,64]{0,1:T(8,128)}) %all-reduce.2.cloned.1.call-update) | async-done | bytes 65552 | tf_op jit(solution)/shard_map/psum | solution.py:69
  294.4 2.0 fusion.20
  296.4 20.3 %all_to_all.24 = bf16[8,128,64]{1,2,0:T(8,128)(2,1)S(1)} all-to-all(bf16[8,128,64]{1,2,0:T(8,128)(2,1)S(1)} %copy.26), channel_id=1, replica_groups=mesh['dom'=64,'head'=8] {'head'}, dimensions={0} | all-to-all | bytes 262144 | tf_op jit(solution)/shard_map/all_to_all | solution.py:122
  316.7 0.9 convolution_convert_fusion.1
  (29 shorter events, 0.1 us)
Async XLA Ops:
  6.5 310.1 %copy-start = (bf16[512,512]{1,0:T(8,128)(2,1)S(1)}, bf16[512,512]{1,0:T(8,128)(2,1)}, u32[]{:S(2)}) copy-start(bf16[512,512]{1,0:T(8,128)(2,1)} %param.14) | copy-start | bytes 1572868
  6.5 14.8 %copy-start.6 = (s32[8,6]{1,0:T(8,128)S(1)}, s32[8,6]{1,0:T(8,128)}, u32[]{:S(2)}) copy-start(s32[8,6]{1,0:T(8,128)} %param.17) | copy-start | bytes 580
  6.5 15.6 %copy-start.1 = (s32[512]{0:T(512)S(1)}, s32[512]{0:T(512)}, u32[]{:S(2)}) copy-start(s32[512]{0:T(512)} %param.19) | copy-start | bytes 6148
  10.8 13.1 %copy-start.7 = (s32[8]{0:T(128)S(1)}, s32[8]{0:T(128)}, u32[]{:S(2)}) copy-start(s32[8]{0:T(128)} %param.18) | copy-start | bytes 100
  10.8 25.6 %copy-start.5 = (bf16[512,192]{0,1:T(8,128)(2,1)S(1)}, bf16[512,192]{0,1:T(8,128)(2,1)}, u32[]{:S(2)}) copy-start(bf16[512,192]{0,1:T(8,128)(2,1)} %param.13) | copy-start | bytes 589828
  10.8 25.6 %all-to-all-start = ((bf16[8,128,512]{2,1,0:T(8,128)(2,1)}), bf16[8,128,512]{2,1,0:T(8,128)(2,1)S(1)}, u32[]{:S(2)}, u32[]{:S(2)}) async-start(bf16[8,128,512]{2,1,0:T(8,128)(2,1)} %stack.2), calls=%async_computation | async-start | bytes 2097152 | tf_op jit(solution)/shard_map/all_to_all | solution.py:52
  21.3 273.0 %all-reduce.2.cloned.1.call-start = ((), (), s32[]{:S(2)}) async-start(), calls=%async_computation.2 | async-start | bytes 131072 | tf_op jit(solution)/shard_map/psum | solution.py:69
  22.1 17.6 %copy-start.4 = (f32[1,64,256]{2,1,0:T(8,128)S(1)}, f32[1,64,256]{2,1,0:T(8,128)}, u32[]{:S(2)}) copy-start(f32[1,64,256]{2,1,0:T(8,128)} %param.15) | copy-start | bytes 196612
  37.0 128.2 %collective-permute-start = (bf16[1024,128]{0,1:T(8,128)(2,1)S(1)}, bf16[1024,128]{0,1:T(8,128)(2,1)S(1)}, u32[]{:S(2)}, u32[]{:S(2)}) collective-permute-start(bf16[1024,128]{0,1:T(8,128)(2,1)S(1)} %bitcast.150), channel_id=1, source_target_pairs={{0,8},{8,16},{16,24},{24,32},{32,40},{40,48},{48,56},{56,64},{64,7... | collective-permute-start | bytes 786440 | tf_op jit(solution)/shard_map/ppermute | solution.py:15
  38.3 126.9 %collective-permute-start.1 = (bf16[1024,128]{0,1:T(8,128)(2,1)S(1)}, bf16[1024,128]{0,1:T(8,128)(2,1)S(1)}, u32[]{:S(2)}, u32[]{:S(2)}) collective-permute-start(bf16[1024,128]{0,1:T(8,128)(2,1)S(1)} %bitcast.151), channel_id=1, source_target_pairs={{8,0},{16,8},{24,16},{32,24},{40,32},{48,40},{56,48},{64,56},{72,6... | collective-permute-start | bytes 786440 | tf_op jit(solution)/shard_map/ppermute | solution.py:18
  169.4 4.4 %copy-start.3 = (bf16[8,8,8,128]{3,2,1,0:T(8,128)(2,1)S(1)}, bf16[8,8,8,128]{3,2,1,0:T(8,128)(2,1)}, u32[]{:S(2)}) copy-start(bf16[8,8,8,128]{3,2,1,0:T(8,128)(2,1)} %copy.30) | copy-start | bytes 393220
  173.8 1.6 copy-start.2
Sparse Core Ops, SparseCore 0:
  44.1 250.2 all-reduce.1
